TPU v7x, 256 devices: a whole 4x4x8 slice. The times are simulated.
256 devices in a mesh: gx: 8 (over x, z_hi), gy: 8 (over z_lo, core), gz: 4 (over y).
Axes of the slice: x: 4, y: 4, z: 8 (z_hi: 2, z_lo: 4; z = z_hi * 4 + z_lo), core: 2. Of those that a mesh axis runs over, the one named last changes fastest.
Arguments:
- cell_index: int32 [3, 8, 8, 4, 1024], P(None, 'gx', 'gy', 'gz'), may hold values from 0 to 127, as said below
- cell_offset: float32 [3, 8, 8, 4, 1024], P(None, 'gx', 'gy', 'gz'), may hold values from 0 to 1
- radius: float32 [8, 8, 4, 1024], P('gx', 'gy', 'gz'), may hold values from 0.3 to 0.7
- forcing: float32 [3, 8, 8, 4, 1024], P(None, 'gx', 'gy', 'gz'), may hold values from -6 to 6
- viscosity: float32 [8, 8, 4, 1024], P('gx', 'gy', 'gz'), may hold values from 0.2 to 2
- occupied: int32 [8, 8, 4, 1024], P('gx', 'gy', 'gz'), may hold values 0 or 1
- base_viscosity: float32 [128, 256, 512], P('gx', 'gy', 'gz'), may hold values from 0.5 to 2
- pair_local: int32 [8, 8, 4, 4096], P('gx', 'gy', 'gz'), may hold values from 0 to 1023
- pair_owner: int32 [8, 8, 4, 4096], P('gx', 'gy', 'gz'), may hold values from 0 to 26
- pair_partner: int32 [8, 8, 4, 4096], P('gx', 'gy', 'gz'), may hold values from 0 to 1023
- pair_slot_mask: int32 [8, 8, 4, 4096], P('gx', 'gy', 'gz'), may hold values 0 or 1
Outputs:
- velocity_field: float32 [3, 128, 256, 512], P(None, 'gx', 'gy', 'gz')
- sphere_velocity: float32 [3, 8, 8, 4, 1024], P(None, 'gx', 'gy', 'gz')
Inputs may be any that keep to these rules, and one draw needn't show every extreme that they name: `cell_index`: row 0 is below 16, row 1 below 32, row 2 below 128.
All inputs are finite; a program needn't handle non-finite values. No bound on the sum of `occupied` or of `pair_slot_mask` on one device may be relied on, other than what follows from the above.
Results may differ from a plain program's by a relative error of at most 0.0003.
Values sent between devices are 32-bit elements; how exact they have to be, the bound alone decides.
A program may use at most 128 MiB of HBM per device.

v0:
```python
import functools
import jax
import jax.numpy as jnp
from jax import lax
from jax.experimental import pallas as pl
from jax.experimental.pallas import tpu as pltpu
from jax.sharding import PartitionSpec as P

spread_sigma = 0.8
damping = 0.5
lubrication_strength = 8.0
minimum_gap = 4.0
sharpness = 1.0 / (2.0 * spread_sigma * spread_sigma)

CX, CY, CZ = 16, 32, 128
SLOTS = 1024
PAIRS = 4096
QB = 512
REACH = 5
PLANES = 28
ROWS = 48
ROW0 = 6
BF = jnp.bfloat16
F32 = jnp.float32
NT = (((1,), (1,)), ((), ()))
NN = (((1,), (0,)), ((), ()))


def halves(value):
    high = value.astype(BF)
    return high, (value - high.astype(F32)).astype(BF)


def dot(a, b, dims):
    return lax.dot_general(a, b, dims, preferred_element_type=F32)


def iota(shape, dim):
    return lax.broadcasted_iota(jnp.int32, shape, dim)


def pairs_kernel(s_ref, zs_ref, q_ref, bucket_ref, self_ref, tab, mtab, acc):
    def parts(v):
        high = v.astype(BF).astype(F32)
        return jnp.concatenate([high, v - high], axis=0).astype(BF)

    for b in range(9):
        t = parts(s_ref[b, 0:8, :])
        for h in range(4):
            tab[pl.ds((b * 4 + h) * 16, 16), :] = t[:, h * 256:(h + 1) * 256]
    for l in range(3):
        t = parts(s_ref[4, 0:8, :] if l == 0 else zs_ref[l - 1, 0:8, :])
        for h in range(4):
            mtab[l, pl.ds(h * 16, 16), :] = t[:, h * 256:(h + 1) * 256]
    acc[...] = jnp.zeros_like(acc)
    self_ref[...] = jnp.zeros_like(self_ref)

    def step(it, carry):
        l = it // (PAIRS // QB)
        ch = it % (PAIRS // QB)
        loc = q_ref[l, 0, pl.ds(ch, 1), :]
        own = q_ref[l, 1, pl.ds(ch, 1), :]
        par = q_ref[l, 2, pl.ds(ch, 1), :]
        live = q_ref[l, 3, pl.ds(ch, 1), :]
        one = lambda c: jnp.where(c, 1, 0)
        dx = one(own >= 9) + one(own >= 18)
        rest = own - 9 * dx
        dy = one(rest >= 3) + one(rest >= 6)
        dz = rest - 3 * dy
        want = jnp.where(l == 0, 1, jnp.where(l == 1, 2, 0))
        brick = dx * 3 + dy
        high_p, low_p = par // 256, par % 256
        high_a, low_a = loc // 256, loc % 256
        rows = iota((256, QB), 0)
        hot_p = jnp.where(rows == low_p, 1.0, 0.0).astype(BF)
        hot_a = jnp.where(rows == low_a, 1.0, 0.0).astype(BF)
        found = dot(tab[...], hot_p, NN)
        slab = jnp.broadcast_to(brick * 4 + high_p, (16, QB))
        other = jnp.zeros((16, QB), F32)
        for k in range(36):
            other = other + jnp.where(slab == k, found[k * 16:(k + 1) * 16], 0.0)
        found_a = dot(mtab[l], hot_a, NN)
        slab_a = jnp.broadcast_to(high_a, (16, QB))
        mine = jnp.zeros((16, QB), F32)
        for k in range(4):
            mine = mine + jnp.where(slab_a == k, found_a[k * 16:(k + 1) * 16], 0.0)
        other = other[0:8] + other[8:16]
        mine = mine[0:8] + mine[8:16]
        diff = other - mine
        r = [
            diff[c:c + 1] + diff[3 + c:4 + c] + (code - 1).astype(F32) * float(side)
            for c, (code, side) in enumerate(((dx, CX), (dy, CY), (dz, CZ)))
        ]
        spacing = jnp.sqrt(r[0] * r[0] + r[1] * r[1] + r[2] * r[2])
        clearance = spacing - mine[6:7] - other[6:7]
        weight = (
            jnp.where(dz == want, live, 0).astype(F32) * mine[7:8] * other[7:8] * lubrication_strength
            / (jnp.maximum(spacing, 1.0) * jnp.maximum(clearance, minimum_gap))
        )
        push = [v * weight for v in r]

        def spread_rows(key, count):
            index = iota((count, QB), 0)
            out = jnp.where(index == key, push[0], 0.0)
            out = jnp.where(index == key + 4, push[1], out)
            out = jnp.where(index == key + 8, push[2], out)
            return halves(out)

        high, low = spread_rows(brick * 12 + high_p, 112)
        acc[...] -= dot(high, hot_p, NT) + dot(low, hot_p, NT)
        high, low = spread_rows(high_a, 16)
        both = dot(high, hot_a, NT) + dot(low, hot_a, NT)
        self_ref[l] += both
        return carry

    lax.fori_loop(0, 3 * (PAIRS // QB), step, 0)
    for b in range(9):
        bucket_ref[b] = acc[b * 12:(b + 1) * 12, :]


def run_pairs(spheres, z_spheres, pairs):
    return pl.pallas_call(
        pairs_kernel,
        out_shape=(
            jax.ShapeDtypeStruct((9, 12, 256), F32),
            jax.ShapeDtypeStruct((3, 16, 256), F32),
        ),
        in_specs=[pl.BlockSpec(memory_space=pltpu.VMEM)] * 3,
        out_specs=(pl.BlockSpec(memory_space=pltpu.VMEM),) * 2,
        scratch_shapes=[
            pltpu.VMEM((576, 256), BF),
            pltpu.VMEM((3, 64, 256), BF),
            pltpu.VMEM((112, 256), F32),
        ],
        compiler_params=pltpu.CompilerParams(vmem_limit_bytes=40 * 2**20),
        name="pairs",
    )(spheres, z_spheres, pairs)


def gauss(shift, offset):
    t = shift + 0.5 - offset
    return jnp.exp(-(t * t) * sharpness)


def norm(offset):
    total = gauss(-2.0, offset)
    for k in range(-1, 3):
        total = total + gauss(float(k), offset)
    return total


def window(cells, target, offset):
    shift = target.astype(F32) - cells
    return jnp.where(jnp.abs(shift) <= 2.0, gauss(shift, offset), 0.0)


X_PARTS = {-1: (0, 7), 0: (3, 20), 1: (19, 7)}
Y_PARTS = {-1: (0, 8), 0: (0, 40), 1: (32, 16)}


def spread_kernel(s_ref, load_ref, main_ref, edge_ref, send_ref, p_high, p_low):
    main_ref[...] = jnp.zeros_like(main_ref)
    edge_ref[...] = jnp.zeros_like(edge_ref)
    line = iota((128, 1), 0)
    code = line % 64
    side = code // 32
    comp = code // 8 % 4
    k = code % 8
    edge_z = jnp.where(
        line < 64,
        jnp.where(side == 0, -5 + k, 125 + k),
        jnp.where(side == 0, -3 + k, 123 + k),
    )

    def brick(dx, dy, x0, nx):
        r0, ny = Y_PARTS[dy]

        def chunk(kc, carry):
            b = (dx + 1) * 3 + (dy + 1)
            s = s_ref[b, kc]
            offs = [s[3 + c:4 + c] for c in range(3)]
            dx_cells = jnp.asarray(dx * CX, jnp.int32).astype(F32)
            wx = window(s[0:1] + dx_cells, iota((nx, 256), 0) + (x0 - REACH), offs[0])
            wy = window(s[1:2] + float(dy * CY), iota((ny, 256), 0) + (r0 - ROW0), offs[1])
            scale = s[7:8] / (norm(offs[0]) * norm(offs[1]) * norm(offs[2]))
            load = [load_ref[b, pl.ds(c * 4 + kc, 1), :] * scale for c in range(3)]
            load.append(s[8:9] * scale)
            for x in range(nx):
                high, low = halves(wx[x:x + 1] * wy)
                p_high[x * ny:(x + 1) * ny] = high
                p_low[x * ny:(x + 1) * ny] = low
            ph, pw = p_high[0:nx * ny], p_low[0:nx * ny]
            wz = window(s[2:3], iota((128, 256), 0), offs[2])
            wedge = window(s[2:3], edge_z, offs[2])
            for c in range(5):
                if c < 4:
                    d = wz * load[c]
                else:
                    d = wedge * jnp.where(
                        comp == 0, load[0], jnp.where(comp == 1, load[1], jnp.where(comp == 2, load[2], load[3]))
                    )
                dh, dl = halves(d)
                res = dot(ph, dh, NT) + dot(pw, dh, NT) + dot(ph, dl, NT)
                res = res.reshape(nx, ny, 128)
                if c < 4:
                    main_ref[c, pl.ds(x0, nx), r0:r0 + ny, :] += res
                else:
                    edge_ref[pl.ds(x0, nx), r0:r0 + ny, :] += res
            return carry

        lax.fori_loop(0, 4, chunk, 0)

    def sided(it, carry):
        dx = 2 * it - 1
        x0 = it * 19
        for dy in (-1, 0, 1):
            brick(dx, dy, x0, 7)
        return carry

    for dy in (-1, 0, 1):
        brick(0, dy, 3, 20)
    lax.fori_loop(0, 2, sided, 0)

    lane = iota((ROWS, 128), 1)

    def pack(g, carry):
        for s in range(2):
            out = jnp.zeros((ROWS, 128), F32)
            for j in range(4):
                rolled = pltpu.roll(edge_ref[g * 4 + j], (32 * j - 64 - 32 * s) % 128, 1) if (32 * j - 64 - 32 * s) % 128 else edge_ref[g * 4 + j]
                out = jnp.where(lane // 32 == j, rolled, out)
            send_ref[s, g] = out
        return carry

    lax.fori_loop(0, PLANES // 4, pack, 0)


def run_spread(spheres, loads):
    return pl.pallas_call(
        spread_kernel,
        out_shape=(
            jax.ShapeDtypeStruct((4, PLANES, ROWS, 128), F32),
            jax.ShapeDtypeStruct((PLANES, ROWS, 128), F32),
            jax.ShapeDtypeStruct((2, PLANES // 4, ROWS, 128), F32),
        ),
        in_specs=[pl.BlockSpec(memory_space=pltpu.VMEM)] * 2,
        out_specs=(pl.BlockSpec(memory_space=pltpu.VMEM),) * 3,
        scratch_shapes=[pltpu.VMEM((800, 256), BF), pltpu.VMEM((800, 256), BF)],
        compiler_params=pltpu.CompilerParams(vmem_limit_bytes=48 * 2**20),
        name="spread",
    )(spheres, loads)


def roll(value, shift, axis):
    shift = shift % value.shape[axis]
    return pltpu.roll(value, shift, axis) if shift else value


def sweep_kernel(
    main_ref, edge_ref, low_ref, high_ref, base_ref, base_edge_ref, s_ref,
    out_ref, vel_ref,
    ua, ub, ha, hb, drive, visco, inv, hdrive, hvisco, hinv, lh, ll,
):
    lane = iota((ROWS, 128), 1)
    comp = lane // 8 % 4

    def start(g, carry):
        from_low, from_high = low_ref[g], high_ref[g]
        for j in range(4):
            i = g * 4 + j
            got = jnp.where(lane < 32, roll(from_low, -32 * j, 1), 0.0)
            got = jnp.where(lane // 32 == 1, roll(from_high, 32 - 32 * j, 1), got)
            total = jnp.where(lane < 64, edge_ref[i], 0.0) + got
            v = total + base_edge_ref[i]
            v = jnp.where(
                comp == 3, v, jnp.where(comp == 2, roll(v, -8, 1), jnp.where(comp == 1, roll(v, -16, 1), roll(v, -24, 1)))
            )
            hvisco[i] = v
            r = 1.0 / (damping + 6.0 * v)
            hinv[i] = r
            hdrive[i] = total
            ha[i] = total * r
            m = []
            for c in range(4):
                near = jnp.where(lane < 2, roll(got, -(c * 8 + 5), 1), 0.0)
                near = jnp.where(lane >= 126, roll(got, 93 - 8 * c, 1), near)
                m.append(main_ref[c, i] + near)
            v = m[3] + base_ref[i]
            visco[i] = v
            r = 1.0 / (damping + 6.0 * v)
            inv[i] = r
            for c in range(3):
                drive[c, i] = m[c]
                ua[c, i] = m[c] * r
        return carry

    lax.fori_loop(0, PLANES // 4, start, 0)

    def sweep(src, dst, hsrc, hdst, first):
        def plane(i, carry):
            h = hsrc[i]
            beside = hsrc[i - 1] + hsrc[i + 1] + roll(h, 1, 0) + roll(h, -1, 0) + roll(h, 1, 1) + roll(h, -1, 1)
            hdst[i] = (hdrive[i] + hvisco[i] * beside) * hinv[i]
            v, r = visco[i], inv[i]
            for c in range(3):
                u = src[c, i]
                before = jnp.where(lane == 0, roll(h, -(c * 8 + 4), 1), roll(u, 1, 1))
                after = jnp.where(lane == 127, roll(h, 92 - 8 * c, 1), roll(u, -1, 1))
                beside = src[c, i - 1] + src[c, i + 1] + roll(u, 1, 0) + roll(u, -1, 0) + before + after
                dst[c, i] = (drive[c, i] + v * beside) * r
            return carry

        lax.fori_loop(first, 26 - first, plane, 0)

    sweep(ua, ub, ha, hb, 1)
    sweep(ub, ua, hb, ha, 2)
    sweep(ua, ub, ha, hb, 3)

    def finish(x, carry):
        for c in range(3):
            out_ref[c, x] = ub[c, x + REACH, ROW0:ROW0 + CY, :]
        return carry

    lax.fori_loop(0, CX, finish, 0)

    comp40 = comp[0:40]

    def gather_rows(x, carry):
        h = hb[x + 3, 0:40, :]
        at = pl.multiple_of(x * 40, 40)
        for c in range(3):
            row = jnp.concatenate([ub[c, x + 3, 0:40, :], jnp.where(comp40 == c, h, 0.0)], axis=1)
            high, low = halves(row)
            lh[c, x] = high.reshape(40, 256)
            ll[c, x] = low.reshape(40, 256)
        return carry

    lax.fori_loop(0, 20, gather_rows, 0)
    line = iota((256, 1), 0)
    code = line - 128
    zed = jnp.where(code < 32, -5 + code % 8, 125 + code % 8)
    zed = jnp.where((zed >= 0) & (zed < CZ) | (code >= 64), -1000, zed)
    zed = jnp.where(line < 128, line, zed)

    for pc in range(4):
        s = s_ref[:, pc * 256:(pc + 1) * 256]
        offs = [s[3 + c:4 + c] for c in range(3)]
        wx = window(s[0:1], iota((20, 256), 0) - 2, offs[0])
        wy = window(s[1:2], iota((40, 256), 0) - ROW0, offs[1])
        wh, wl = halves(window(s[2:3], zed, offs[2]))
        scale = s[7:8] / (norm(offs[0]) * norm(offs[1]) * norm(offs[2]))
        for c in range(3):
            a, b = lh[c].reshape(800, 256), ll[c].reshape(800, 256)
            g = dot(a, wh, NN) + dot(b, wh, NN) + dot(a, wl, NN)
            t = jnp.zeros((40, 256), F32)
            for x in range(20):
                t = t + wx[x:x + 1] * g[x * 40:(x + 1) * 40]
            vel_ref[c:c + 1, pc * 256:(pc + 1) * 256] = jnp.sum(t * wy, axis=0, keepdims=True) * scale


def run_sweeps(main, edge, low, high, base, base_edge, sphere):
    field = lambda *lead: pltpu.VMEM(lead + (PLANES, ROWS, 128), F32)
    return pl.pallas_call(
        sweep_kernel,
        out_shape=(
            jax.ShapeDtypeStruct((3, CX, CY, CZ), F32),
            jax.ShapeDtypeStruct((3, SLOTS), F32),
        ),
        in_specs=[pl.BlockSpec(memory_space=pltpu.VMEM)] * 7,
        out_specs=(pl.BlockSpec(memory_space=pltpu.VMEM),) * 2,
        scratch_shapes=[
            field(3), field(3), field(), field(), field(3), field(), field(), field(), field(), field(),
            pltpu.VMEM((3, 20, 40, 256), BF), pltpu.VMEM((3, 20, 40, 256), BF),
        ],
        compiler_params=pltpu.CompilerParams(vmem_limit_bytes=56 * 2**20),
        name="sweeps",
    )(main, edge, low, high, base, base_edge, sphere)


def shift(value, axis, step):
    size = lax.axis_size(axis)
    return lax.ppermute(value, axis, [(i, (i + step) % size) for i in range(size)])


def around(value, axis, dim):
    return jnp.concatenate([shift(value, axis, 1), value, shift(value, axis, -1)], axis=dim)


def halo(array, axis, dim, width):
    n = array.shape[dim]
    before = shift(lax.slice_in_dim(array, n - width, n, axis=dim), axis, 1)
    after = shift(lax.slice_in_dim(array, 0, width, axis=dim), axis, -1)
    return before, after


def body(
    cell_index, cell_offset, radius, forcing, viscosity, occupied, base_viscosity,
    pair_local, pair_owner, pair_partner, pair_slot_mask,
):
    row = lambda a: a.reshape(-1, SLOTS)
    sphere = jnp.concatenate(
        [
            row(cell_index).astype(F32), row(cell_offset), row(radius),
            row(occupied).astype(F32), row(viscosity),
        ],
        0,
    )
    pairs = jnp.stack(
        [a.reshape(PAIRS // QB, QB) for a in (pair_local, pair_owner, pair_partner, pair_slot_mask)]
    )
    spheres = around(around(sphere[None], "gx", 0)[:, None], "gy", 1).reshape(9, 9, SLOTS)
    z_spheres = jnp.stack([shift(sphere[:8], "gz", 1), shift(sphere[:8], "gz", -1)])
    all_pairs = jnp.stack([pairs, shift(pairs, "gz", 1), shift(pairs, "gz", -1)])

    before, after = halo(base_viscosity, "gx", 0, REACH)
    base = jnp.concatenate([before, base_viscosity, after], 0)
    before, after = halo(base, "gy", 1, REACH)
    base = jnp.concatenate([before, base, after], 1)
    base = jnp.pad(base, ((0, PLANES - 26), (ROW0 - REACH, ROWS - ROW0 - REACH - CY), (0, 0)))
    before, after = halo(base, "gz", 2, REACH)
    blank = lambda n: jnp.zeros((PLANES, ROWS, n), F32)
    base_edge = jnp.concatenate(
        [blank(24), before, base[:, :, 0:3], blank(24), base[:, :, CZ - 3:CZ], after, blank(64)], 2
    )

    bucket, selves = run_pairs(spheres, z_spheres, all_pairs)
    selves = selves[:, :12]
    bucket = bucket.reshape(3, 3, 12, 256)
    bucket = bucket[:, 1] + shift(bucket[:, 2], "gy", 1) + shift(bucket[:, 0], "gy", -1)
    total = bucket[1] + shift(bucket[2], "gx", 1) + shift(bucket[0], "gx", -1)
    total = total + forcing.reshape(12, 256) + selves[0] + shift(selves[1], "gz", -1) + shift(selves[2], "gz", 1)
    loads = around(around(total[None], "gx", 0)[:, None], "gy", 1).reshape(9, 12, 256)

    chunked = spheres.reshape(9, 9, 4, 256).transpose(0, 2, 1, 3)
    main, edge, send = run_spread(chunked, loads)
    high = shift(send[0], "gz", -1)
    low = shift(send[1], "gz", 1)
    field, velocity = run_sweeps(main, edge, low, high, base, base_edge, sphere)
    return field, velocity.reshape(3, 1, 1, 1, SLOTS)


def solution(mesh):
    line = P("gx", "gy", "gz", None)
    wide = P(None, "gx", "gy", "gz", None)
    placed = (wide, wide, line, wide, line, line, P("gx", "gy", "gz"), line, line, line, line)
    return jax.shard_map(
        body,
        mesh=mesh,
        in_specs=placed,
        out_specs=(P(None, "gx", "gy", "gz"), wide),
        check_vma=False,
    )
```

profile of v0, /device:TPU:1, one launch (start us, length us, event | category | flops | bytes accessed | tf_op | source)
XLA Modules:
  0.0 171.4 jit_solution(4986178035046051913)
XLA Ops:
  0.6 0.7 convert_bitcast_fusion
  1.3 0.7 fusion.11
  2.0 0.7 copy.60
  2.7 0.7 pad_maximum_fusion.3
  3.5 3.6 %collective-permute-start.5 = (f32[8,1024]{1,0:T(8,128)S(1)}, f32[8,1024]{1,0:T(8,128)S(1)}, u32[]{:S(2)}, u32[]{:S(2)}) collective-permute-start(f32[8,1024]{1,0:T(8,128)S(1)} %pad_maximum_fusion.3), channel_id=1, source_target_pairs={{0,3},{1,0},{2,1},{3,2},{4,7},{5,4},{6,5},{7,6},{8,11},{9,8},{10,9... | collective-permute-start | bytes 98312 | tf_op jit(solution)/shard_map/ppermute | solution.py:382
  7.1 0.7 constant_dynamic-update-slice_fusion.3
  7.8 0.7 constant_dynamic-update-slice_fusion.2
  8.5 0.7 constant_dynamic-update-slice_fusion.1
  9.3 0.7 constant_dynamic-update-slice_fusion
  10.0 2.7 %collective-permute-start.7 = (s32[4,8,512]{2,1,0:T(8,128)S(1)}, s32[4,8,512]{2,1,0:T(8,128)S(1)}, u32[]{:S(2)}, u32[]{:S(2)}) collective-permute-start(s32[4,8,512]{2,1,0:T(8,128)S(1)} %constant_dynamic-update-slice_fusion), channel_id=1, source_target_pairs={{0,3},{1,0},{2,1},{3,2},{4,7},{5,4},{6,5},{7,6},{8,11},{9,8},{10,9... | collective-permute-start | bytes 196616 | tf_op jit(solution)/shard_map/ppermute | solution.py:382
  12.7 1.4 concatenate.27.s_ref
  14.1 9.2 %collective-permute-start.1 = (f32[1,9,1024]{2,1,0:T(8,128)S(1)}, f32[1,9,1024]{2,1,0:T(8,128)S(1)}, u32[]{:S(2)}, u32[]{:S(2)}) collective-permute-start(f32[1,9,1024]{2,1,0:T(8,128)S(1)} %bitcast.97), channel_id=1, source_target_pairs={{0,224},{32,0},{64,32},{96,64},{128,96},{160,128},{192,160},{224,1... | collective-permute-start | bytes 110600 | tf_op jit(solution)/shard_map/ppermute | solution.py:382
  23.2 0.9 fusion.15
  24.2 0.7 reduce.4
  25.1 7.5 %collective-permute-start.21 = (f32[5,32,128]{2,1,0:T(8,128)S(1)}, f32[5,32,128]{2,1,0:T(8,128)S(1)}, u32[]{:S(2)}, u32[]{:S(2)}) collective-permute-start(f32[5,32,128]{2,1,0:T(8,128)S(1)} %get-tuple-element.30), channel_id=1, source_target_pairs={{0,224},{32,0},{64,32},{96,64},{128,96},{160,128},{192,160},{224,1... | collective-permute-start | bytes 245768 | tf_op jit(solution)/shard_map/ppermute | solution.py:382
  32.6 2.2 %collective-permute-done = f32[1,9,1024]{2,1,0:T(8,128)S(1)} collective-permute-done((f32[1,9,1024]{2,1,0:T(8,128)S(1)}, f32[1,9,1024]{2,1,0:T(8,128)S(1)}, u32[]{:S(2)}, u32[]{:S(2)}) %collective-permute-start) | collective-permute-done | bytes 36896 | tf_op jit(solution)/shard_map/ppermute | solution.py:382
  34.9 2.4 %collective-permute-start.3 = (f32[3,1,9,1024]{3,2,0,1:T(8,128)S(1)}, f32[3,1,9,1024]{3,2,0,1:T(8,128)S(1)}, u32[]{:S(2)}, u32[]{:S(2)}) collective-permute-start(f32[3,1,9,1024]{3,2,0,1:T(8,128)S(1)} %maximum_bitcast_fusion), channel_id=1, source_target_pairs={{0,28},{4,0},{8,4},{12,8},{16,12},{20,16},{24,20},{28,24},{1,29},{... | collective-permute-start | bytes 331784 | tf_op jit(solution)/shard_map/ppermute | solution.py:382
  37.3 2.7 %collective-permute-start.2 = (f32[3,1,9,1024]{3,2,0,1:T(8,128)S(1)}, f32[3,1,9,1024]{3,2,0,1:T(8,128)S(1)}, u32[]{:S(2)}, u32[]{:S(2)}) collective-permute-start(f32[3,1,9,1024]{3,2,0,1:T(8,128)S(1)} %maximum_bitcast_fusion), channel_id=1, source_target_pairs={{0,4},{4,8},{8,12},{12,16},{16,20},{20,24},{24,28},{28,0},{1,5},{5... | collective-permute-start | bytes 331784 | tf_op jit(solution)/shard_map/ppermute | solution.py:382
  40.0 2.4 %collective-permute-done.20 = f32[5,32,128]{2,1,0:T(8,128)S(1)} collective-permute-done((f32[5,32,128]{2,1,0:T(8,128)S(1)}, f32[5,32,128]{2,1,0:T(8,128)S(1)}, u32[]{:S(2)}, u32[]{:S(2)}) %collective-permute-start.20) | collective-permute-done | bytes 81952 | tf_op jit(solution)/shard_map/ppermute | solution.py:382
  42.4 1.0 constant_dynamic-update-slice_fusion.5
  43.4 2.4 %collective-permute-done.3 = f32[3,1,9,1024]{3,2,0,1:T(8,128)S(1)} collective-permute-done((f32[3,1,9,1024]{3,2,0,1:T(8,128)S(1)}, f32[3,1,9,1024]{3,2,0,1:T(8,128)S(1)}, u32[]{:S(2)}, u32[]{:S(2)}) %collective-permute-start.3) | collective-permute-done | bytes 110624 | tf_op jit(solution)/shard_map/ppermute | solution.py:382
  45.8 20.4 %pairs.1 = (f32[9,12,256]{2,1,0:T(8,128)S(1)}, f32[3,16,256]{2,1,0:T(8,128)S(1)}) custom-call(f32[9,9,1024]{2,1,0:T(8,128)S(1)} %bitcast.93, f32[2,8,1024]{2,1,0:T(8,128)S(1)} %pad_maximum_fusion.2.zs_ref, s32[3,4,8,512]{3,2,1,0:T(8,128)S(1)} %pad_add_fusion.q_ref), custom_call_target="tpu_custom_call" | custom-call | tf_op jit(solution)/shard_map/pairs/pallas_call | solution.py:122
  66.3 1.5 collective-permute-start.8
  67.8 3.0 %collective-permute-start.12 = (f32[12,256]{1,0:T(8,128)S(1)}, f32[12,256]{1,0:T(8,128)S(1)}, u32[]{:S(2)}, u32[]{:S(2)}) collective-permute-start(f32[12,256]{1,0:T(8,128)S(1)} %get-tuple-element.36), channel_id=1, source_target_pairs={{0,3},{1,0},{2,1},{3,2},{4,7},{5,4},{6,5},{7,6},{8,11},{9,8},{10,9... | collective-permute-start | bytes 36872 | tf_op jit(solution)/shard_map/ppermute | solution.py:382
  70.8 0.8 collective-permute-done.9
  71.6 1.4 collective-permute-start.10
  73.0 6.4 %collective-permute-start.11 = (f32[12,256]{1,0:T(8,128)S(1)}, f32[12,256]{1,0:T(8,128)S(1)}, u32[]{:S(2)}, u32[]{:S(2)}) collective-permute-start(f32[12,256]{1,0:T(8,128)S(1)} %get-tuple-element.35), channel_id=1, source_target_pairs={{0,224},{32,0},{64,32},{96,64},{128,96},{160,128},{192,160},{224,1... | collective-permute-start | bytes 36872 | tf_op jit(solution)/shard_map/ppermute | solution.py:382
  79.4 1.9 %collective-permute-start.22 = (f32[26,5,128]{2,1,0:T(8,128)S(1)}, f32[26,5,128]{2,1,0:T(8,128)S(1)}, u32[]{:S(2)}, u32[]{:S(2)}) collective-permute-start(f32[26,5,128]{2,1,0:T(8,128)S(1)} %get-tuple-element.26), channel_id=1, source_target_pairs={{0,4},{4,8},{8,12},{12,16},{16,20},{20,24},{24,28},{28,0},{1,5},{5... | collective-permute-start | bytes 199688 | tf_op jit(solution)/shard_map/ppermute | solution.py:382
  81.9 1.5 collective-permute-start.23
  83.5 4.6 %collective-permute-start.15 = (f32[1,12,256]{2,1,0:T(8,128)S(1)}, f32[1,12,256]{2,1,0:T(8,128)S(1)}, u32[]{:S(2)}, u32[]{:S(2)}) collective-permute-start(f32[1,12,256]{2,1,0:T(8,128)S(1)} %fusion.10), channel_id=1, source_target_pairs={{0,224},{32,0},{64,32},{96,64},{128,96},{160,128},{192,160},{224,1... | collective-permute-start | bytes 36872 | tf_op jit(solution)/shard_map/ppermute | solution.py:382
  88.1 0.9 collective-permute-start.14
  89.1 1.0 collective-permute-done.15
  90.1 6.6 %collective-permute-done.14 = f32[1,12,256]{2,1,0:T(8,128)S(1)} collective-permute-done((f32[1,12,256]{2,1,0:T(8,128)S(1)}, f32[1,12,256]{2,1,0:T(8,128)S(1)}, u32[]{:S(2)}, u32[]{:S(2)}) %collective-permute-start.14) | collective-permute-done | bytes 12320 | tf_op jit(solution)/shard_map/ppermute | solution.py:382
  96.7 5.8 %collective-permute-start.17 = (f32[3,1,12,256]{3,2,0,1:T(8,128)S(1)}, f32[3,1,12,256]{3,2,0,1:T(8,128)S(1)}, u32[]{:S(2)}, u32[]{:S(2)}) collective-permute-start(f32[3,1,12,256]{3,2,0,1:T(8,128)S(1)} %maximum_bitcast_fusion.1), channel_id=1, source_target_pairs={{0,28},{4,0},{8,4},{12,8},{16,12},{20,16},{24,20},{28,24},{1,29},{... | collective-permute-start | bytes 110600 | tf_op jit(solution)/shard_map/ppermute | solution.py:382
  102.7 0.3 copy.36
  103.0 0.3 copy.35
  103.4 3.2 %collective-permute-start.25 = (f32[28,48,5]{1,0,2:T(8,128)S(1)}, f32[28,48,5]{1,0,2:T(8,128)S(1)}, u32[]{:S(2)}, u32[]{:S(2)}) collective-permute-start(f32[28,48,5]{1,0,2:T(8,128)S(1)} %copy.36), channel_id=1, source_target_pairs={{0,3},{1,0},{2,1},{3,2},{4,7},{5,4},{6,5},{7,6},{8,11},{9,8},{10,9... | collective-permute-start | bytes 80648 | tf_op jit(solution)/shard_map/ppermute | solution.py:382
  106.7 29.2 %spread.1 = (f32[4,28,48,128]{3,2,1,0:T(8,128)S(1)}, f32[28,48,128]{2,1,0:T(8,128)S(1)}, f32[2,7,48,128]{3,2,1,0:T(8,128)S(1)}) custom-call(f32[9,4,9,256]{3,2,1,0:T(8,128)S(1)} %bitcast.92, f32[9,12,256]{2,1,0:T(8,128)S(1)} %bitcast.94), custom_call_target="tpu_custom_call" | custom-call | tf_op jit(solution)/shard_map/spread/pallas_call | solution.py:239
  136.0 1.5 copy-done
  137.5 0.9 copy-done.1
  138.3 0.8 slice_bitcast_fusion
  139.1 1.2 collective-permute-start.19
  140.2 0.3 collective-permute-start.18
  141.1 1.2 copy.37
  142.3 0.9 broadcast_in_dim.19
  143.3 3.8 %concatenate.35.base_edge_ref = f32[28,48,128]{2,1,0:T(8,128)} concatenate(f32[28,48,24]{2,1,0:T(8,128)S(1)} %broadcast.5, f32[28,48,5]{2,1,0:T(8,128)} %copy.37, f32[28,48,3]{2,1,0:T(8,128)S(1)} %get-tuple-element.25, f32[28,48,24]{2,1,0:T(8,128)S(1)} %broadcast.5, f32[28,48,3]{2,1,0:T(8,128)S(1)} %get-tuple-element.24, f32[28,48,5]{2,1,0:T(8,128)S(1)} %copy.38, ...), dimensions={2} | concatenate | bytes 1376256 | tf_op jit(solution)/shard_map/concatenate | solution.py:422
  147.0 23.0 %sweeps.1 = (f32[3,16,32,128]{3,2,1,0:T(8,128)}, f32[3,1024]{1,0:T(4,128)}) custom-call(f32[4,28,48,128]{3,2,1,0:T(8,128)} %copy-done, f32[28,48,128]{2,1,0:T(8,128)} %copy-done.1, f32[7,48,128]{2,1,0:T(8,128)} %collective-permute-done.18.low_ref, f32[7,48,128]{2,1,0:T(8,128)} %collective-permute-done.19.high_ref, f32[28,48,128]{2,1,0:T(8,128)} %copy-done.2, ...), custom_call_target="tpu_custom_call" | custom-call | tf_op jit(solution)/shard_map/sweeps/pallas_call | solution.py:363
  170.1 1.3 copy.39
  (59 shorter events, 2.1 us)
Async XLA Ops:
  3.5 21.5 %collective-permute-start.5 = (f32[8,1024]{1,0:T(8,128)S(1)}, f32[8,1024]{1,0:T(8,128)S(1)}, u32[]{:S(2)}, u32[]{:S(2)}) collective-permute-start(f32[8,1024]{1,0:T(8,128)S(1)} %pad_maximum_fusion.3), channel_id=1, source_target_pairs={{0,3},{1,0},{2,1},{3,2},{4,7},{5,4},{6,5},{7,6},{8,11},{9,8},{10,9... | collective-permute-start | bytes 98312 | tf_op jit(solution)/shard_map/ppermute | solution.py:382
  7.1 18.0 %collective-permute-start.4 = (f32[8,1024]{1,0:T(8,128)S(1)}, f32[8,1024]{1,0:T(8,128)S(1)}, u32[]{:S(2)}, u32[]{:S(2)}) collective-permute-start(f32[8,1024]{1,0:T(8,128)S(1)} %pad_maximum_fusion.3), channel_id=1, source_target_pairs={{0,1},{1,2},{2,3},{3,0},{4,5},{5,6},{6,7},{7,4},{8,9},{9,10},{10,1... | collective-permute-start | bytes 98312 | tf_op jit(solution)/shard_map/ppermute | solution.py:382
  10.0 27.3 %collective-permute-start.7 = (s32[4,8,512]{2,1,0:T(8,128)S(1)}, s32[4,8,512]{2,1,0:T(8,128)S(1)}, u32[]{:S(2)}, u32[]{:S(2)}) collective-permute-start(s32[4,8,512]{2,1,0:T(8,128)S(1)} %constant_dynamic-update-slice_fusion), channel_id=1, source_target_pairs={{0,3},{1,0},{2,1},{3,2},{4,7},{5,4},{6,5},{7,6},{8,11},{9,8},{10,9... | collective-permute-start | bytes 196616 | tf_op jit(solution)/shard_map/ppermute | solution.py:382
  12.6 27.3 %collective-permute-start.6 = (s32[4,8,512]{2,1,0:T(8,128)S(1)}, s32[4,8,512]{2,1,0:T(8,128)S(1)}, u32[]{:S(2)}, u32[]{:S(2)}) collective-permute-start(s32[4,8,512]{2,1,0:T(8,128)S(1)} %constant_dynamic-update-slice_fusion), channel_id=1, source_target_pairs={{0,1},{1,2},{2,3},{3,0},{4,5},{5,6},{6,7},{7,4},{8,9},{9,10},{10,1... | collective-permute-start | bytes 196616 | tf_op jit(solution)/shard_map/ppermute | solution.py:382
  14.1 52.2 %copy-start.3 = (f32[9,1024]{1,0:T(8,128)}, f32[9,1024]{1,0:T(8,128)S(1)}, u32[]{:S(2)}) copy-start(f32[9,1024]{1,0:T(8,128)S(1)} %concatenate.27.s_ref) | copy-start | bytes 110596
  14.1 18.5 %collective-permute-start.1 = (f32[1,9,1024]{2,1,0:T(8,128)S(1)}, f32[1,9,1024]{2,1,0:T(8,128)S(1)}, u32[]{:S(2)}, u32[]{:S(2)}) collective-permute-start(f32[1,9,1024]{2,1,0:T(8,128)S(1)} %bitcast.97), channel_id=1, source_target_pairs={{0,224},{32,0},{64,32},{96,64},{128,96},{160,128},{192,160},{224,1... | collective-permute-start | bytes 110600 | tf_op jit(solution)/shard_map/ppermute | solution.py:382
  25.0 9.9 %collective-permute-start = (f32[1,9,1024]{2,1,0:T(8,128)S(1)}, f32[1,9,1024]{2,1,0:T(8,128)S(1)}, u32[]{:S(2)}, u32[]{:S(2)}) collective-permute-start(f32[1,9,1024]{2,1,0:T(8,128)S(1)} %bitcast.98), channel_id=1, source_target_pairs={{0,32},{32,64},{64,96},{96,128},{128,160},{160,192},{192,224},{224... | collective-permute-start | bytes 110600 | tf_op jit(solution)/shard_map/ppermute | solution.py:382
  25.1 18.3 %collective-permute-start.21 = (f32[5,32,128]{2,1,0:T(8,128)S(1)}, f32[5,32,128]{2,1,0:T(8,128)S(1)}, u32[]{:S(2)}, u32[]{:S(2)}) collective-permute-start(f32[5,32,128]{2,1,0:T(8,128)S(1)} %get-tuple-element.30), channel_id=1, source_target_pairs={{0,224},{32,0},{64,32},{96,64},{128,96},{160,128},{192,160},{224,1... | collective-permute-start | bytes 245768 | tf_op jit(solution)/shard_map/ppermute | solution.py:382
  32.5 9.8 %collective-permute-start.20 = (f32[5,32,128]{2,1,0:T(8,128)S(1)}, f32[5,32,128]{2,1,0:T(8,128)S(1)}, u32[]{:S(2)}, u32[]{:S(2)}) collective-permute-start(f32[5,32,128]{2,1,0:T(8,128)S(1)} %get-tuple-element.31), channel_id=1, source_target_pairs={{0,32},{32,64},{64,96},{96,128},{128,160},{160,192},{192,224},{224... | collective-permute-start | bytes 245768 | tf_op jit(solution)/shard_map/ppermute | solution.py:382
  34.9 10.9 %collective-permute-start.3 = (f32[3,1,9,1024]{3,2,0,1:T(8,128)S(1)}, f32[3,1,9,1024]{3,2,0,1:T(8,128)S(1)}, u32[]{:S(2)}, u32[]{:S(2)}) collective-permute-start(f32[3,1,9,1024]{3,2,0,1:T(8,128)S(1)} %maximum_bitcast_fusion), channel_id=1, source_target_pairs={{0,28},{4,0},{8,4},{12,8},{16,12},{20,16},{24,20},{28,24},{1,29},{... | collective-permute-start | bytes 331784 | tf_op jit(solution)/shard_map/ppermute | solution.py:382
  37.3 8.5 %collective-permute-start.2 = (f32[3,1,9,1024]{3,2,0,1:T(8,128)S(1)}, f32[3,1,9,1024]{3,2,0,1:T(8,128)S(1)}, u32[]{:S(2)}, u32[]{:S(2)}) collective-permute-start(f32[3,1,9,1024]{3,2,0,1:T(8,128)S(1)} %maximum_bitcast_fusion), channel_id=1, source_target_pairs={{0,4},{4,8},{8,12},{12,16},{16,20},{20,24},{24,28},{28,0},{1,5},{5... | collective-permute-start | bytes 331784 | tf_op jit(solution)/shard_map/ppermute | solution.py:382
  66.3 4.5 %collective-permute-start.8 = (f32[3,12,256]{2,1,0:T(8,128)S(1)}, f32[3,12,256]{2,1,0:T(8,128)S(1)}, u32[]{:S(2)}, u32[]{:S(2)}) collective-permute-start(f32[3,12,256]{2,1,0:T(8,128)S(1)} %get-tuple-element.32), channel_id=1, source_target_pairs={{0,4},{4,8},{8,12},{12,16},{16,20},{20,24},{24,28},{28,0},{1,5},{5... | collective-permute-start | bytes 110600 | tf_op jit(solution)/shard_map/ppermute | solution.py:382
  67.8 3.8 %collective-permute-start.9 = (f32[3,12,256]{2,1,0:T(8,128)S(1)}, f32[3,12,256]{2,1,0:T(8,128)S(1)}, u32[]{:S(2)}, u32[]{:S(2)}) collective-permute-start(f32[3,12,256]{2,1,0:T(8,128)S(1)} %get-tuple-element.33), channel_id=1, source_target_pairs={{0,28},{4,0},{8,4},{12,8},{16,12},{20,16},{24,20},{28,24},{1,29},{... | collective-permute-start | bytes 110600 | tf_op jit(solution)/shard_map/ppermute | solution.py:382
  67.8 14.1 %collective-permute-start.12 = (f32[12,256]{1,0:T(8,128)S(1)}, f32[12,256]{1,0:T(8,128)S(1)}, u32[]{:S(2)}, u32[]{:S(2)}) collective-permute-start(f32[12,256]{1,0:T(8,128)S(1)} %get-tuple-element.36), channel_id=1, source_target_pairs={{0,3},{1,0},{2,1},{3,2},{4,7},{5,4},{6,5},{7,6},{8,11},{9,8},{10,9... | collective-permute-start | bytes 36872 | tf_op jit(solution)/shard_map/ppermute | solution.py:382
  70.8 12.7 %collective-permute-start.13 = (f32[12,256]{1,0:T(8,128)S(1)}, f32[12,256]{1,0:T(8,128)S(1)}, u32[]{:S(2)}, u32[]{:S(2)}) collective-permute-start(f32[12,256]{1,0:T(8,128)S(1)} %get-tuple-element.37), channel_id=1, source_target_pairs={{0,1},{1,2},{2,3},{3,0},{4,5},{5,6},{6,7},{7,4},{8,9},{9,10},{10,1... | collective-permute-start | bytes 36872 | tf_op jit(solution)/shard_map/ppermute | solution.py:382
  71.6 11.8 %collective-permute-start.10 = (f32[12,256]{1,0:T(8,128)S(1)}, f32[12,256]{1,0:T(8,128)S(1)}, u32[]{:S(2)}, u32[]{:S(2)}) collective-permute-start(f32[12,256]{1,0:T(8,128)S(1)} %get-tuple-element.34), channel_id=1, source_target_pairs={{0,32},{32,64},{64,96},{96,128},{128,160},{160,192},{192,224},{224... | collective-permute-start | bytes 36872 | tf_op jit(solution)/shard_map/ppermute | solution.py:382
  73.0 10.5 %collective-permute-start.11 = (f32[12,256]{1,0:T(8,128)S(1)}, f32[12,256]{1,0:T(8,128)S(1)}, u32[]{:S(2)}, u32[]{:S(2)}) collective-permute-start(f32[12,256]{1,0:T(8,128)S(1)} %get-tuple-element.35), channel_id=1, source_target_pairs={{0,224},{32,0},{64,32},{96,64},{128,96},{160,128},{192,160},{224,1... | collective-permute-start | bytes 36872 | tf_op jit(solution)/shard_map/ppermute | solution.py:382
  79.4 9.5 %collective-permute-start.22 = (f32[26,5,128]{2,1,0:T(8,128)S(1)}, f32[26,5,128]{2,1,0:T(8,128)S(1)}, u32[]{:S(2)}, u32[]{:S(2)}) collective-permute-start(f32[26,5,128]{2,1,0:T(8,128)S(1)} %get-tuple-element.26), channel_id=1, source_target_pairs={{0,4},{4,8},{8,12},{12,16},{16,20},{20,24},{24,28},{28,0},{1,5},{5... | collective-permute-start | bytes 199688 | tf_op jit(solution)/shard_map/ppermute | solution.py:382
  81.9 7.0 %collective-permute-start.23 = (f32[26,5,128]{2,1,0:T(8,128)S(1)}, f32[26,5,128]{2,1,0:T(8,128)S(1)}, u32[]{:S(2)}, u32[]{:S(2)}) collective-permute-start(f32[26,5,128]{2,1,0:T(8,128)S(1)} %get-tuple-element.27), channel_id=1, source_target_pairs={{0,28},{4,0},{8,4},{12,8},{16,12},{20,16},{24,20},{28,24},{1,29},{... | collective-permute-start | bytes 199688 | tf_op jit(solution)/shard_map/ppermute | solution.py:382
  83.5 6.6 %collective-permute-start.15 = (f32[1,12,256]{2,1,0:T(8,128)S(1)}, f32[1,12,256]{2,1,0:T(8,128)S(1)}, u32[]{:S(2)}, u32[]{:S(2)}) collective-permute-start(f32[1,12,256]{2,1,0:T(8,128)S(1)} %fusion.10), channel_id=1, source_target_pairs={{0,224},{32,0},{64,32},{96,64},{128,96},{160,128},{192,160},{224,1... | collective-permute-start | bytes 36872 | tf_op jit(solution)/shard_map/ppermute | solution.py:382
  88.1 8.6 %collective-permute-start.14 = (f32[1,12,256]{2,1,0:T(8,128)S(1)}, f32[1,12,256]{2,1,0:T(8,128)S(1)}, u32[]{:S(2)}, u32[]{:S(2)}) collective-permute-start(f32[1,12,256]{2,1,0:T(8,128)S(1)} %fusion.10), channel_id=1, source_target_pairs={{0,32},{32,64},{64,96},{96,128},{128,160},{160,192},{192,224},{224... | collective-permute-start | bytes 36872 | tf_op jit(solution)/shard_map/ppermute | solution.py:382
  89.1 51.5 %copy-start.2 = (f32[28,48,128]{2,1,0:T(8,128)}, f32[28,48,128]{2,1,0:T(8,128)S(1)}, u32[]{:S(2)}) copy-start(f32[28,48,128]{2,1,0:T(8,128)S(1)} %select_maximum_fusion.base_ref) | copy-start | bytes 2064388
  96.7 10.0 %collective-permute-start.17 = (f32[3,1,12,256]{3,2,0,1:T(8,128)S(1)}, f32[3,1,12,256]{3,2,0,1:T(8,128)S(1)}, u32[]{:S(2)}, u32[]{:S(2)}) collective-permute-start(f32[3,1,12,256]{3,2,0,1:T(8,128)S(1)} %maximum_bitcast_fusion.1), channel_id=1, source_target_pairs={{0,28},{4,0},{8,4},{12,8},{16,12},{20,16},{24,20},{28,24},{1,29},{... | collective-permute-start | bytes 110600 | tf_op jit(solution)/shard_map/ppermute | solution.py:382
  102.4 4.2 %collective-permute-start.16 = (f32[3,1,12,256]{3,2,0,1:T(8,128)S(1)}, f32[3,1,12,256]{3,2,0,1:T(8,128)S(1)}, u32[]{:S(2)}, u32[]{:S(2)}) collective-permute-start(f32[3,1,12,256]{3,2,0,1:T(8,128)S(1)} %maximum_bitcast_fusion.1), channel_id=1, source_target_pairs={{0,4},{4,8},{8,12},{12,16},{16,20},{20,24},{24,28},{28,0},{1,5},{5... | collective-permute-start | bytes 110600 | tf_op jit(solution)/shard_map/ppermute | solution.py:382
  103.3 37.8 %collective-permute-start.24 = (f32[28,48,5]{1,0,2:T(8,128)S(1)}, f32[28,48,5]{1,0,2:T(8,128)S(1)}, u32[]{:S(2)}, u32[]{:S(2)}) collective-permute-start(f32[28,48,5]{1,0,2:T(8,128)S(1)} %copy.35), channel_id=1, source_target_pairs={{0,1},{1,2},{2,3},{3,0},{4,5},{5,6},{6,7},{7,4},{8,9},{9,10},{10,1... | collective-permute-start | bytes 80648 | tf_op jit(solution)/shard_map/ppermute | solution.py:382
  103.4 37.4 %collective-permute-start.25 = (f32[28,48,5]{1,0,2:T(8,128)S(1)}, f32[28,48,5]{1,0,2:T(8,128)S(1)}, u32[]{:S(2)}, u32[]{:S(2)}) collective-permute-start(f32[28,48,5]{1,0,2:T(8,128)S(1)} %copy.36), channel_id=1, source_target_pairs={{0,3},{1,0},{2,1},{3,2},{4,7},{5,4},{6,5},{7,6},{8,11},{9,8},{10,9... | collective-permute-start | bytes 80648 | tf_op jit(solution)/shard_map/ppermute | solution.py:382
  136.0 1.5 copy-start
  137.5 0.9 copy-start.1
  139.1 7.9 %collective-permute-start.19 = (f32[7,48,128]{2,1,0:T(8,128)}, f32[7,48,128]{2,1,0:T(8,128)}, u32[]{:S(2)}, u32[]{:S(2)}) collective-permute-start(f32[7,48,128]{2,1,0:T(8,128)} %get-tuple-element.28), channel_id=1, source_target_pairs={{0,3},{1,0},{2,1},{3,2},{4,7},{5,4},{6,5},{7,6},{8,11},{9,8},{10,9... | collective-permute-start | bytes 516104 | tf_op jit(solution)/shard_map/ppermute | solution.py:382
  140.2 6.8 %collective-permute-start.18 = (f32[7,48,128]{2,1,0:T(8,128)}, f32[7,48,128]{2,1,0:T(8,128)}, u32[]{:S(2)}, u32[]{:S(2)}) collective-permute-start(f32[7,48,128]{2,1,0:T(8,128)} %get-tuple-element.29), channel_id=1, source_target_pairs={{0,1},{1,2},{2,3},{3,0},{4,5},{5,6},{6,7},{7,4},{8,9},{9,10},{10,1... | collective-permute-start | bytes 516104 | tf_op jit(solution)/shard_map/ppermute | solution.py:382
where the time goes:
time: 174 us; the launch traced here: 171 us
  Pallas kernels  72.6 us (42%)
  starting transfers between devices  59.9 us (34%)
  local copies, waits for them, and re-layouts  19.4 us (11%)
  waiting for transfers between devices  15.5 us (9%)
  other arithmetic  3.08 us (2%)
    ppermute x26, starting transfers between devices, shift(): lax.ppermute(value, axis, [(i, (i + step) % size) for i in range(size)])  59.9 us
    pallas_call x1, Pallas kernels, run_spread(): pl.pallas_call(spread_kernel, out_shape=(jax.ShapeDtypeStruct((4, PLANES,...  29.2 us
    pallas_call x1, Pallas kernels, run_sweeps(): pl.pallas_call(sweep_kernel, out_shape=(jax.ShapeDtypeStruct((3, CX, CY,...  23 us
    pallas_call x1, Pallas kernels, run_pairs(): pl.pallas_call(pairs_kernel, out_shape=(jax.ShapeDtypeStruct((9, 12, 256)...  20.4 us
    ppermute x26, waiting for transfers between devices, shift(): lax.ppermute(value, axis, [(i, (i + step) % size) for i in range(size)])  15.5 us
    unnamed x15, local copies, waits for them, and re-layouts  7.54 us
    concatenate x1, local copies, waits for them, and re-layouts, body(): jnp.concatenate([blank(24), before, base[:, :, 0:3], blank(24), base[:, :...  3.76 us
  transfers between devices with their start and end apart: 26, of which 6 were waited for; matrix products, arithmetic and copies ran while one was open for 9% of the time, Pallas kernels for 17%

commit v1 on v0

v1 whole, which is shorter than its diff:
```python
import functools
import jax
import jax.numpy as jnp
from jax import lax
from jax.experimental import pallas as pl
from jax.experimental.pallas import tpu as pltpu
from jax.sharding import PartitionSpec as P

spread_sigma = 0.8
damping = 0.5
lubrication_strength = 8.0
minimum_gap = 4.0
sharpness = 1.0 / (2.0 * spread_sigma * spread_sigma)

CX, CY, CZ = 16, 32, 128
SLOTS = 1024
PAIRS = 4096
QB = 512
REACH = 5
PLANES = 28
ROWS = 48
ROW0 = 6
BF = jnp.bfloat16
F32 = jnp.float32
NT = (((1,), (1,)), ((), ()))
NN = (((1,), (0,)), ((), ()))


def halves(value):
    high = value.astype(BF)
    return high, (value - high.astype(F32)).astype(BF)


def dot(a, b, dims):
    return lax.dot_general(a, b, dims, preferred_element_type=F32)


def iota(shape, dim):
    return lax.broadcasted_iota(jnp.int32, shape, dim)


def gauss(shift, offset):
    t = shift + 0.5 - offset
    return jnp.exp(-(t * t) * sharpness)


def norm(offset):
    total = gauss(-2.0, offset)
    for k in range(-1, 3):
        total = total + gauss(float(k), offset)
    return total


def window(cells, target, offset):
    shift = target.astype(F32) - cells
    return jnp.where(jnp.abs(shift) <= 2.0, gauss(shift, offset), 0.0)


def roll(value, shift, axis):
    shift = shift % value.shape[axis]
    return pltpu.roll(value, shift, axis) if shift else value


X_PARTS = {-1: (0, 7), 0: (3, 20), 1: (19, 7)}
Y_PARTS = {-1: (0, 8), 0: (0, 40), 1: (32, 16)}


def pair_forces(s, zs, q, acc, selves, tab, mtab):
    def parts(v):
        high = v.astype(BF).astype(F32)
        return jnp.concatenate([high, v - high], axis=0).astype(BF)

    def fill(n, carry):
        tab[pl.ds(pl.multiple_of(n * 16, 16), 16), :] = parts(s[n // 4, n % 4])
        return carry

    lax.fori_loop(0, 36, fill, 0)
    for h in range(4):
        mtab[0, h * 16:(h + 1) * 16] = parts(s[4, h])
        mtab[1, h * 16:(h + 1) * 16] = parts(zs[0, h])
        mtab[2, h * 16:(h + 1) * 16] = parts(zs[1, h])
    acc[...] = jnp.zeros_like(acc)
    selves[...] = jnp.zeros_like(selves)

    def step(it, carry):
        l = it // (PAIRS // QB)
        ch = it % (PAIRS // QB)
        loc = q[l, 0, pl.ds(ch, 1), :]
        own = q[l, 1, pl.ds(ch, 1), :]
        par = q[l, 2, pl.ds(ch, 1), :]
        live = q[l, 3, pl.ds(ch, 1), :]
        one = lambda c: jnp.where(c, 1, 0)
        dx = one(own >= 9) + one(own >= 18)
        rest = own - 9 * dx
        dy = one(rest >= 3) + one(rest >= 6)
        dz = rest - 3 * dy
        want = jnp.where(l == 0, 1, jnp.where(l == 1, 2, 0))
        brick = dy * 3 + dx
        high_p, low_p = par // 256, par % 256
        high_a, low_a = loc // 256, loc % 256
        rows = iota((256, QB), 0)
        hot_p = jnp.where(rows == low_p, 1.0, 0.0).astype(BF)
        hot_a = jnp.where(rows == low_a, 1.0, 0.0).astype(BF)
        found = dot(tab[...], hot_p, NN)
        slab = jnp.broadcast_to(brick * 4 + high_p, (16, QB))
        other = jnp.zeros((16, QB), F32)
        for k in range(36):
            other = other + jnp.where(slab == k, found[k * 16:(k + 1) * 16], 0.0)
        found_a = dot(mtab[l], hot_a, NN)
        slab_a = jnp.broadcast_to(high_a, (16, QB))
        mine = jnp.zeros((16, QB), F32)
        for k in range(4):
            mine = mine + jnp.where(slab_a == k, found_a[k * 16:(k + 1) * 16], 0.0)
        other = other[0:8] + other[8:16]
        mine = mine[0:8] + mine[8:16]
        diff = other - mine
        r = [
            diff[c:c + 1] + diff[3 + c:4 + c] + (code - 1).astype(F32) * float(side)
            for c, (code, side) in enumerate(((dx, CX), (dy, CY), (dz, CZ)))
        ]
        spacing = jnp.sqrt(r[0] * r[0] + r[1] * r[1] + r[2] * r[2])
        clearance = spacing - mine[6:7] - other[6:7]
        weight = (
            jnp.where(dz == want, live, 0).astype(F32) * mine[7:8] * other[7:8] * lubrication_strength
            / (jnp.maximum(spacing, 1.0) * jnp.maximum(clearance, minimum_gap))
        )
        push = [v * weight for v in r]

        def spread_rows(key, count):
            index = iota((count, QB), 0)
            out = jnp.where(index == key, push[0], 0.0)
            out = jnp.where(index == key + 4, push[1], out)
            out = jnp.where(index == key + 8, push[2], out)
            return halves(out)

        high, low = spread_rows(brick * 12 + high_p, 112)
        acc[...] -= dot(high, hot_p, NT) + dot(low, hot_p, NT)
        high, low = spread_rows(high_a, 16)
        selves[l] += dot(high, hot_a, NT) + dot(low, hot_a, NT)
        return carry

    lax.fori_loop(0, 3 * (PAIRS // QB), step, 0)


def spread_brick(s, loads, main, edge, p_high, p_low, dx, dy, x0, nx):
    r0, ny = Y_PARTS[dy]
    line = iota((128, 1), 0)
    code = line % 64
    side = code // 32
    comp = code // 8 % 4
    k = code % 8
    edge_z = jnp.where(
        line < 64,
        jnp.where(side == 0, -5 + k, 125 + k),
        jnp.where(side == 0, -3 + k, 123 + k),
    )
    b = (dy + 1) * 3 + (dx + 1)

    def chunk(kc, carry):
        v = s[b, kc]
        offs = [v[3 + c:4 + c] for c in range(3)]
        dx_cells = jnp.asarray(dx * CX, jnp.int32).astype(F32)
        wx = window(v[0:1] + dx_cells, iota((nx, 256), 0) + (x0 - REACH), offs[0])
        wy = window(v[1:2] + float(dy * CY), iota((ny, 256), 0) + (r0 - ROW0), offs[1])
        scale = 1.0 / (norm(offs[0]) * norm(offs[1]) * norm(offs[2]))
        load = [loads[b, pl.ds(c * 4 + kc, 1), :] * scale for c in range(4)]
        for x in range(nx):
            high, low = halves(wx[x:x + 1] * wy)
            p_high[x * ny:(x + 1) * ny] = high
            p_low[x * ny:(x + 1) * ny] = low
        ph, pw = p_high[0:nx * ny], p_low[0:nx * ny]
        wz = window(v[2:3], iota((128, 256), 0), offs[2])
        wedge = window(v[2:3], edge_z, offs[2])
        for c in range(5):
            if c < 4:
                d = wz * load[c]
            else:
                d = wedge * jnp.where(
                    comp == 0, load[0], jnp.where(comp == 1, load[1], jnp.where(comp == 2, load[2], load[3]))
                )
            dh, dl = halves(d)
            res = dot(ph, dh, NT) + dot(pw, dh, NT) + dot(ph, dl, NT)
            res = res.reshape(nx, ny, 128)
            if c < 4:
                main[c, pl.ds(x0, nx), r0:r0 + ny, :] += res
            else:
                edge[pl.ds(x0, nx), r0:r0 + ny, :] += res
        return carry

    lax.fori_loop(0, 4, chunk, 0)


def assemble_base(bx, by, i):
    rows = jnp.concatenate([by[0, i], bx[i], by[1, i]], axis=0)
    return pltpu.roll(rows, ROWS - (8 - ROW0), 0)


def exchange_kernel(
    cell_ref, offset_ref, radius_ref, force_ref, visc_ref, live_ref, base_ref,
    local_ref, owner_ref, partner_ref, mask_ref,
    main, edge, rim, bx_out, by_out, own_ref,
    s, zs, q, acc, selves, tab, mtab, ry, rz, xb, rx, loads, pack, force, got, p_high, p_low,
    bx, by, send_sem, recv_sem,
):
    me = {a: lax.axis_index(a) for a in ("gx", "gy", "gz")}

    def near(axis, step):
        n = lax.axis_size(axis)
        return {axis: lax.rem(me[axis] + step + n, n)}

    barrier = pltpu.get_barrier_semaphore()
    for axis in ("gx", "gy", "gz"):
        for step in (1, -1):
            pl.semaphore_signal(barrier, inc=1, device_id=near(axis, step), device_id_type=pl.DeviceIdType.MESH)

    count = [0]

    def copy(src, dst, axis, step):
        n = count[0]
        count[0] += 1
        return pltpu.make_async_remote_copy(
            src_ref=src, dst_ref=dst, send_sem=send_sem.at[n], recv_sem=recv_sem.at[n],
            device_id=near(axis, step), device_id_type=pl.DeviceIdType.MESH,
        )

    rows = [cell_ref[c, 0, 0].astype(F32) for c in range(3)] + [offset_ref[c, 0, 0] for c in range(3)]
    rows += [radius_ref[0, 0], live_ref[0, 0].astype(F32)]
    for r, v in enumerate(rows):
        for h in range(4):
            s[4, h, r:r + 1, :] = v[:, h * 256:(h + 1) * 256]
    for j, ref in enumerate((local_ref, owner_ref, partner_ref, mask_ref)):
        for ch in range(PAIRS // QB):
            q[0, j, ch:ch + 1, :] = ref[0, 0, :, ch * QB:(ch + 1) * QB]
    bx[REACH:REACH + CX] = base_ref[...]
    bx[26:28] = jnp.zeros((2, CY, CZ), F32)

    pl.semaphore_wait(barrier, 6)

    s_x = [copy(s.at[4], s.at[3], "gx", 1), copy(s.at[4], s.at[5], "gx", -1)]
    s_z = [copy(s.at[4], zs.at[0], "gz", 1), copy(s.at[4], zs.at[1], "gz", -1)]
    q_z = [copy(q.at[0], q.at[1], "gz", 1), copy(q.at[0], q.at[2], "gz", -1)]
    b_x = [
        copy(bx.at[pl.ds(CX, REACH)], bx.at[pl.ds(0, REACH)], "gx", 1),
        copy(bx.at[pl.ds(REACH, REACH)], bx.at[pl.ds(CX + REACH, REACH)], "gx", -1),
    ]
    s_y = [copy(s.at[pl.ds(3, 3)], s.at[pl.ds(0, 3)], "gy", 1), copy(s.at[pl.ds(3, 3)], s.at[pl.ds(6, 3)], "gy", -1)]
    b_y = [
        copy(bx.at[:, pl.ds(CY - 8, 8)], by.at[0], "gy", 1),
        copy(bx.at[:, pl.ds(0, 8)], by.at[1], "gy", -1),
    ]
    a_y = [copy(acc.at[pl.ds(72, 40)], ry.at[0], "gy", 1), copy(acc.at[pl.ds(0, 40)], ry.at[1], "gy", -1)]
    a_z = [copy(selves.at[1], rz.at[0], "gz", -1), copy(selves.at[2], rz.at[1], "gz", 1)]
    a_x = [copy(xb.at[1], rx.at[0], "gx", 1), copy(xb.at[0], rx.at[1], "gx", -1)]
    l_x = [copy(loads.at[4], loads.at[3], "gx", 1), copy(loads.at[4], loads.at[5], "gx", -1)]
    l_y = [
        copy(loads.at[pl.ds(3, 3)], loads.at[pl.ds(0, 3)], "gy", 1),
        copy(loads.at[pl.ds(3, 3)], loads.at[pl.ds(6, 3)], "gy", -1),
    ]
    e_z = [copy(pack.at[0], got.at[1], "gz", -1), copy(pack.at[1], got.at[0], "gz", 1)]

    def start(copies):
        for c in copies:
            c.start()

    def arrived(copies):
        for c in copies:
            c.wait_recv()

    start(s_x)
    start(s_z)
    start(q_z)
    start(b_x)

    own_ref[...] = s[4]
    force[...] = jnp.zeros_like(force)
    loads[4] = jnp.zeros((16, 256), F32)
    for c in range(3):
        for h in range(4):
            force[c * 4 + h:c * 4 + h + 1, :] = force_ref[c, 0, 0, :, h * 256:(h + 1) * 256]
    thick = visc_ref[0, 0] * live_ref[0, 0].astype(F32)
    for h in range(4):
        force[12 + h:13 + h, :] = thick[:, h * 256:(h + 1) * 256]
    main[...] = jnp.zeros_like(main)
    edge[...] = jnp.zeros_like(edge)

    arrived(s_x)
    start(s_y)
    arrived(b_x)
    start(b_y)
    arrived(s_z)
    arrived(q_z)
    arrived(s_y)

    pair_forces(s, zs, q, acc, selves, tab, mtab)

    start(a_y)
    start(a_z)
    arrived(a_y)
    middle = acc[36:72] + ry[0, 0:36] + ry[1, 0:36]
    xb[...] = jnp.zeros_like(xb)
    xb[0, 0:12] = middle[0:12]
    xb[1, 0:12] = middle[24:36]
    start(a_x)
    arrived(a_z)
    force[0:12] += middle[12:24] + selves[0, 0:12] + rz[0, 0:12] + rz[1, 0:12]
    arrived(a_x)
    for h in range(4):
        alive = s[4, h, 7:8, :]
        for c in range(3):
            at = c * 4 + h
            loads[4, at:at + 1, :] = alive * (force[at:at + 1] + rx[0, at:at + 1] + rx[1, at:at + 1])
        loads[4, 12 + h:13 + h, :] = force[12 + h:13 + h]
    start(l_x)

    put = functools.partial(spread_brick, s, loads, main, edge, p_high, p_low)
    put(0, 0, 3, 20)
    arrived(l_x)
    start(l_y)
    lax.fori_loop(0, 2, lambda it, carry: (put(2 * it - 1, 0, it * 19, 7), carry)[1], 0)
    arrived(l_y)
    for dy in (-1, 1):
        put(0, dy, 3, 20)
        lax.fori_loop(0, 2, lambda it, carry: (put(2 * it - 1, dy, it * 19, 7), carry)[1], 0)

    arrived(b_y)
    lane = iota((ROWS, 128), 1)

    def wrap(g, carry):
        tiles = []
        for j in range(4):
            i = g * 4 + j
            b = assemble_base(bx, by, i)
            t = edge[i]
            t = t + jnp.where((lane >= 29) & (lane < 32), roll(b, 29, 1), 0.0)
            t = t + jnp.where((lane >= 56) & (lane < 59), roll(b, 56 - 125, 1), 0.0)
            t = t + jnp.where((lane >= 91) & (lane < 96), roll(b, 91, 1), 0.0)
            t = t + jnp.where((lane >= 120) & (lane < 125), roll(b, 120 - 123, 1), 0.0)
            edge[i] = t
            tiles.append(t)
        for side in range(2):
            out = jnp.zeros((ROWS, 128), F32)
            for j in range(4):
                out = jnp.where(lane // 32 == j, roll(tiles[j], 32 * j - 64 - 32 * side, 1), out)
            pack[side, g] = out
        return carry

    lax.fori_loop(0, PLANES // 4, wrap, 0)
    start(e_z)
    arrived(e_z)
    rim[...] = got[...]
    bx_out[...] = bx[...]
    by_out[...] = by[...]
    for group in (s_x, s_z, q_z, b_x, s_y, b_y, a_y, a_z, a_x, l_x, l_y, e_z):
        for c in group:
            c.wait_send()


def run_exchange(*args):
    vmem = pl.BlockSpec(memory_space=pltpu.VMEM)
    shape = lambda *s: jax.ShapeDtypeStruct(s, F32)
    return pl.pallas_call(
        exchange_kernel,
        out_shape=(
            shape(4, PLANES, ROWS, 128),
            shape(PLANES, ROWS, 128),
            shape(2, PLANES // 4, ROWS, 128),
            shape(PLANES, CY, CZ),
            shape(2, PLANES, 8, CZ),
            shape(4, 8, 256),
        ),
        in_specs=[vmem] * 11,
        out_specs=(vmem,) * 6,
        scratch_shapes=[
            pltpu.VMEM((9, 4, 8, 256), F32),
            pltpu.VMEM((2, 4, 8, 256), F32),
            pltpu.VMEM((3, 4, PAIRS // QB, QB), jnp.int32),
            pltpu.VMEM((112, 256), F32),
            pltpu.VMEM((3, 16, 256), F32),
            pltpu.VMEM((576, 256), BF),
            pltpu.VMEM((3, 64, 256), BF),
            pltpu.VMEM((2, 40, 256), F32),
            pltpu.VMEM((2, 16, 256), F32),
            pltpu.VMEM((2, 16, 256), F32),
            pltpu.VMEM((2, 16, 256), F32),
            pltpu.VMEM((9, 16, 256), F32),
            pltpu.VMEM((2, PLANES // 4, ROWS, 128), F32),
            pltpu.VMEM((16, 256), F32),
            pltpu.VMEM((2, PLANES // 4, ROWS, 128), F32),
            pltpu.VMEM((800, 256), BF),
            pltpu.VMEM((800, 256), BF),
            pltpu.VMEM((PLANES, CY, CZ), F32),
            pltpu.VMEM((2, PLANES, 8, CZ), F32),
            pltpu.SemaphoreType.DMA((24,)),
            pltpu.SemaphoreType.DMA((24,)),
        ],
        compiler_params=pltpu.CompilerParams(
            collective_id=0, has_side_effects=True, vmem_limit_bytes=48 * 2**20
        ),
        name="exchange",
    )(*args)


def sweep_kernel(
    main_ref, edge_ref, rim_ref, bx_ref, by_ref, s_ref,
    out_ref, vel_ref,
    ua, ub, ha, hb, drive, visco, inv, hdrive, hvisco, hinv, lh, ll,
):
    lane = iota((ROWS, 128), 1)
    comp = lane // 8 % 4

    def start(g, carry):
        from_low, from_high = rim_ref[0, g], rim_ref[1, g]
        for j in range(4):
            i = g * 4 + j
            got = jnp.where(lane < 32, roll(from_low, -32 * j, 1), 0.0)
            got = jnp.where(lane // 32 == 1, roll(from_high, 32 - 32 * j, 1), got)
            total = jnp.where(lane < 64, edge_ref[i], 0.0) + got
            v = total
            v = jnp.where(
                comp == 3, v, jnp.where(comp == 2, roll(v, -8, 1), jnp.where(comp == 1, roll(v, -16, 1), roll(v, -24, 1)))
            )
            hvisco[i] = v
            r = 1.0 / (damping + 6.0 * v)
            hinv[i] = r
            hdrive[i] = total
            ha[i] = total * r
            m = []
            for c in range(4):
                near = jnp.where(lane < 2, roll(got, -(c * 8 + 5), 1), 0.0)
                near = jnp.where(lane >= 126, roll(got, 93 - 8 * c, 1), near)
                m.append(main_ref[c, i] + near)
            v = m[3] + assemble_base(bx_ref, by_ref, i)
            visco[i] = v
            r = 1.0 / (damping + 6.0 * v)
            inv[i] = r
            for c in range(3):
                drive[c, i] = m[c]
                ua[c, i] = m[c] * r
        return carry

    lax.fori_loop(0, PLANES // 4, start, 0)

    def sweep(src, dst, hsrc, hdst, first):
        def plane(i, carry):
            h = hsrc[i]
            beside = hsrc[i - 1] + hsrc[i + 1] + roll(h, 1, 0) + roll(h, -1, 0) + roll(h, 1, 1) + roll(h, -1, 1)
            hdst[i] = (hdrive[i] + hvisco[i] * beside) * hinv[i]
            v, r = visco[i], inv[i]
            for c in range(3):
                u = src[c, i]
                before = jnp.where(lane == 0, roll(h, -(c * 8 + 4), 1), roll(u, 1, 1))
                after = jnp.where(lane == 127, roll(h, 92 - 8 * c, 1), roll(u, -1, 1))
                beside = src[c, i - 1] + src[c, i + 1] + roll(u, 1, 0) + roll(u, -1, 0) + before + after
                dst[c, i] = (drive[c, i] + v * beside) * r
            return carry

        lax.fori_loop(first, 26 - first, plane, 0)

    sweep(ua, ub, ha, hb, 1)
    sweep(ub, ua, hb, ha, 2)
    sweep(ua, ub, ha, hb, 3)

    def finish(x, carry):
        for c in range(3):
            out_ref[c, x] = ub[c, x + REACH, ROW0:ROW0 + CY, :]
        return carry

    lax.fori_loop(0, CX, finish, 0)

    comp40 = comp[0:40]

    def gather_rows(x, carry):
        h = hb[x + 3, 0:40, :]
        at = pl.multiple_of(x * 40, 40)
        for c in range(3):
            row = jnp.concatenate([ub[c, x + 3, 0:40, :], jnp.where(comp40 == c, h, 0.0)], axis=1)
            high, low = halves(row)
            lh[c, x] = high.reshape(40, 256)
            ll[c, x] = low.reshape(40, 256)
        return carry

    lax.fori_loop(0, 20, gather_rows, 0)
    line = iota((256, 1), 0)
    code = line - 128
    zed = jnp.where(code < 32, -5 + code % 8, 125 + code % 8)
    zed = jnp.where((zed >= 0) & (zed < CZ) | (code >= 64), -1000, zed)
    zed = jnp.where(line < 128, line, zed)

    for pc in range(4):
        s = s_ref[pc]
        offs = [s[3 + c:4 + c] for c in range(3)]
        wx = window(s[0:1], iota((20, 256), 0) - 2, offs[0])
        wy = window(s[1:2], iota((40, 256), 0) - ROW0, offs[1])
        wh, wl = halves(window(s[2:3], zed, offs[2]))
        scale = s[7:8] / (norm(offs[0]) * norm(offs[1]) * norm(offs[2]))
        for c in range(3):
            a, b = lh[c].reshape(800, 256), ll[c].reshape(800, 256)
            g = dot(a, wh, NN) + dot(b, wh, NN) + dot(a, wl, NN)
            t = jnp.zeros((40, 256), F32)
            for x in range(20):
                t = t + wx[x:x + 1] * g[x * 40:(x + 1) * 40]
            vel_ref[c, 0, 0, :, pc * 256:(pc + 1) * 256] = jnp.sum(t * wy, axis=0, keepdims=True) * scale


def run_sweeps(*args):
    field = lambda *lead: pltpu.VMEM(lead + (PLANES, ROWS, 128), F32)
    return pl.pallas_call(
        sweep_kernel,
        out_shape=(
            jax.ShapeDtypeStruct((3, CX, CY, CZ), F32),
            jax.ShapeDtypeStruct((3, 1, 1, 1, SLOTS), F32),
        ),
        in_specs=[pl.BlockSpec(memory_space=pltpu.VMEM)] * 6,
        out_specs=(pl.BlockSpec(memory_space=pltpu.VMEM),) * 2,
        scratch_shapes=[
            field(3), field(3), field(), field(), field(3), field(), field(), field(), field(), field(),
            pltpu.VMEM((3, 20, 40, 256), BF), pltpu.VMEM((3, 20, 40, 256), BF),
        ],
        compiler_params=pltpu.CompilerParams(vmem_limit_bytes=56 * 2**20),
        name="sweeps",
    )(*args)


def body(*args):
    return run_sweeps(*run_exchange(*args))

def solution(mesh):
    line = P("gx", "gy", "gz", None)
    wide = P(None, "gx", "gy", "gz", None)
    placed = (wide, wide, line, wide, line, line, P("gx", "gy", "gz"), line, line, line, line)
    return jax.shard_map(
        body,
        mesh=mesh,
        in_specs=placed,
        out_specs=(P(None, "gx", "gy", "gz"), wide),
        check_vma=False,
    )
```

time: 174 us -> 130 us (0.75)
  starting transfers between devices: 59.9 us -> 0 us
  Pallas kernels: 72.6 us -> 115 us
  waiting for transfers between devices: 15.5 us -> 0 us
  local copies, waits for them, and re-layouts: 19.4 us -> 13.2 us
  other arithmetic: 3.08 us -> 0 us
    ppermute x26 -> x0, starting transfers between devices: 59.9 us -> none  [shift(): lax.ppermute(value, axis, [(i, (i + step) % size) for i in range(size)])]
    pallas_call x2 -> x1, Pallas kernels: 49.6 us -> 92.1 us  [run_exchange(): pl.pallas_call(exchange_kernel, out_shape=(shape(4, PLANES, ROWS, 128), s...]
    ppermute x26 -> x0, waiting for transfers between devices: 15.5 us -> none  [shift(): lax.ppermute(value, axis, [(i, (i + step) % size) for i in range(size)])]
    unnamed x15 -> x34, local copies, waits for them, and re-layouts: 7.54 us -> 13.2 us
    concatenate x5 -> x0, local copies, waits for them, and re-layouts: 5.42 us -> none  [the longest x1 3.76 us: body(): jnp.concatenate([blank(24), before, base[:, :, 0:3], blank(24), base[:, :...]
    slice x6 -> x0, local copies, waits for them, and re-layouts: 2.09 us -> none  [the longest x3 1.5 us: halo(): after = shift(lax.slice_in_dim(array, 0, width, axis=dim), axis, -1)]
  transfers between devices with their start and end apart: 26 -> 0, of which waited for: 6 -> 0; matrix products, arithmetic and copies ran while one was open for 9% -> 0% of each run, Pallas kernels for 17% -> 0%
where the time goes in v1:
time: 130 us; the launch traced here: 129 us
  Pallas kernels  115 us (88%)
  local copies, waits for them, and re-layouts  13.2 us (10%)
    pallas_call x1, Pallas kernels, run_exchange(): pl.pallas_call(exchange_kernel, out_shape=(shape(4, PLANES, ROWS, 128), s...  92.1 us
    pallas_call x1, Pallas kernels, run_sweeps(): pl.pallas_call(sweep_kernel, out_shape=(jax.ShapeDtypeStruct((3, CX, CY,...  22.8 us
    unnamed x34, local copies, waits for them, and re-layouts  13.2 us

profile of v1, /device:TPU:1, one launch (start us, length us, event | category | flops | bytes accessed | tf_op | source)
XLA Modules:
  0.0 128.8 jit_solution(2318696232773590103)
XLA Ops:
  0.6 0.0 copy-start.4
  0.6 0.9 copy-done.4
  1.6 0.0 copy-start.7
  1.6 0.7 copy-done.7
  2.3 0.0 copy-start.8
  2.3 0.7 copy-done.8
  3.0 0.0 copy-start.9
  3.0 0.7 copy-done.9
  3.7 0.0 copy-start.10
  3.7 0.7 copy-done.10
  4.5 0.0 copy-start.11
  4.5 0.7 copy-done.11
  5.2 0.0 copy-start.12
  5.2 0.7 copy-done.12
  5.9 0.0 copy-start.13
  5.9 0.7 copy-done.13
  6.6 0.0 copy-start.14
  6.6 0.7 copy-done.14
  7.3 0.0 copy-start.15
  7.3 0.7 copy-done.15
  8.0 0.0 copy-start.16
  8.0 0.7 copy-done.16
  8.6 92.1 %exchange.1 = (f32[4,28,48,128]{3,2,1,0:T(8,128)S(1)}, f32[28,48,128]{2,1,0:T(8,128)S(1)}, f32[2,7,48,128]{3,2,1,0:T(8,128)S(1)}, f32[28,32,128]{2,1,0:T(8,128)S...) custom-call(s32[3,1,1,1,1024]{4,3,2,1,0:T(1,128)S(1)} %copy-done.11, f32[3,1,1,1,1024]{4,3,2,1,0:T(1,128)S(1)} %copy-done.12, ...), custom_call_target="tpu_custom_call" | custom-call | tf_op jit(solution)/shard_map/exchange/pallas_call | solution.py:361
  100.8 0.0 copy-start
  100.8 1.5 %copy-done = f32[4,28,48,128]{3,2,1,0:T(8,128)} copy-done((f32[4,28,48,128]{3,2,1,0:T(8,128)}, f32[4,28,48,128]{3,2,1,0:T(8,128)S(1)}, u32[]{:S(2)}) %copy-start) | copy-done | bytes 2752536
  102.3 0.0 copy-start.1
  102.3 0.9 copy-done.1
  103.2 0.0 copy-start.2
  103.2 0.8 copy-done.2
  104.0 0.0 copy-start.3
  104.0 0.7 copy-done.3
  104.7 0.0 copy-start.5
  104.7 0.7 copy-done.5
  105.4 0.0 copy-start.6
  105.4 0.6 copy-done.6
  106.0 22.8 %sweeps.1 = (f32[3,16,32,128]{3,2,1,0:T(8,128)}, f32[3,1,1,1,1024]{4,3,2,1,0:T(1,128)}) custom-call(f32[4,28,48,128]{3,2,1,0:T(8,128)} %copy-done, f32[28,48,128]{2,1,0:T(8,128)} %copy-done.1, f32[2,7,48,128]{3,2,1,0:T(8,128)} %copy-done.3, f32[28,32,128]{2,1,0:T(8,128)} %copy-done.2, f32[2,28,8,128]{3,2,1,0:T(8,128)} %copy-done.5, f32[4,8,256]{2,1,0:T(8,128)} %copy-done.6), custom_call_target="tpu_custom_call" | custom-call | tf_op jit(solution)/shard_map/sweeps/pallas_call | solution.py:507
Async XLA Ops:
  0.6 1.0 copy-start.4
  1.6 0.7 copy-start.7
  2.3 0.7 copy-start.8
  3.0 0.7 copy-start.9
  3.7 0.7 copy-start.10
  4.5 0.7 copy-start.11
  5.2 0.7 copy-start.12
  5.9 0.7 copy-start.13
  6.6 0.7 copy-start.14
  7.3 0.7 copy-start.15
  8.0 0.7 copy-start.16
  100.8 1.5 %copy-start = (f32[4,28,48,128]{3,2,1,0:T(8,128)}, f32[4,28,48,128]{3,2,1,0:T(8,128)S(1)}, u32[]{:S(2)}) copy-start(f32[4,28,48,128]{3,2,1,0:T(8,128)S(1)} %get-tuple-element.8.main_ref) | copy-start | bytes 8257540
  102.3 0.9 copy-start.1
  103.2 0.8 copy-start.2
  104.0 0.7 copy-start.3
  104.7 0.7 copy-start.5
  105.4 0.6 copy-start.6
